TPU v7x, 32 devices: a whole 2x2x4 slice. The times are simulated.
32 devices in a mesh: cell: 8 (over z, y), stn: 4 (over x, core).
Axes of the slice: x: 2, y: 2, z: 4, core: 2. Of those that a mesh axis runs over, the one named last changes fastest.
Arguments:
- cell_points: float32 [3, 8192], P(None, 'cell'), may hold values from 0 to 1
- magnetization: float32 [3, 8192], P(None, 'cell'), may hold values from -6 to 6
- cell_level: int32 [8192], P('cell'), may hold values from 0 to 2
- suscept: float32 [8192], P('cell'), may hold values from 0.2 to 2
- inducing: float32 [3], replicated, may hold values from -4 to 4
- stations: float32 [3, 4096], P(None, 'stn'), may hold values from 0 to 2, as said below
Outputs:
- updated: float32 [3, 8192], P(None, ('cell', 'stn'))
- predictions: float32 [4096], P(('stn', 'cell'))
Inputs may be any that keep to these rules, and one draw needn't show every extreme that they name: `stations`: the first two coordinates lie in the unit square; the third is 1 plus 0.5 to 2 times 8192 ** (-1/3).
All inputs are finite; a program needn't handle non-finite values.
Results may differ from a plain program's by a relative error of at most 0.0003.
Values sent between devices are 32-bit elements; how exact they have to be, the bound alone decides.
A program may use at most 64 MiB of HBM per device.

v0:
```python
import math
import jax
import jax.numpy as jnp
from jax import lax
from jax.sharding import PartitionSpec as P

INV_FOUR_PI = 0.25 / math.pi


def block_width(targets, sources):
    ceiling = max(256, (1 << 20) // targets)
    ceiling = 1 << ceiling.bit_length() - 1
    return math.gcd(sources, ceiling)


def pair_field(points, source_piece):
    delta_x = points[0][:, None] - source_piece[0][None, :]
    delta_y = points[1][:, None] - source_piece[1][None, :]
    delta_z = points[2][:, None] - source_piece[2][None, :]
    soften = source_piece[6][None, :]
    radius_sq = delta_x * delta_x + delta_y * delta_y + delta_z * delta_z + soften * soften
    inverse = lax.rsqrt(radius_sq)
    inverse_sq = inverse * inverse
    weight = INV_FOUR_PI * soften * soften * soften * inverse_sq * inverse
    projection = (
        3.0
        * (
            delta_x * source_piece[3][None, :]
            + delta_y * source_piece[4][None, :]
            + delta_z * source_piece[5][None, :]
        )
        * inverse_sq
    )
    field_x = jnp.sum(weight * (projection * delta_x - source_piece[3][None, :]), axis=1)
    field_y = jnp.sum(weight * (projection * delta_y - source_piece[4][None, :]), axis=1)
    field_z = jnp.sum(weight * (projection * delta_z - source_piece[5][None, :]), axis=1)
    return jnp.stack([field_x, field_y, field_z], 0)


def source_field(points, sources):
    number = sources.shape[1]
    blockw = block_width(points.shape[1], number)
    groups = sources.reshape(7, number // blockw, blockw).transpose(1, 0, 2)

    def advance(summed, source_piece):
        return (summed + pair_field(points, source_piece), None)

    result, unused = lax.scan(advance, jnp.zeros((3, points.shape[1]), jnp.float32), groups)
    return result


def shards(cell_points, magnetization, cell_level, suscept, inducing, stations):
    cycle_size = lax.axis_size("cell")
    section = lax.axis_size("stn")
    block_cells = cell_points.shape[1]
    spacing = float(block_cells * cycle_size * section // section) ** (-1.0 / 3.0)
    size_h = spacing * jnp.power(0.5, cell_level.astype(jnp.float32))
    packed = jnp.concatenate([cell_points, magnetization, size_h[None, :]], 0)
    owned = block_cells // section
    offset = lax.axis_index("stn") * owned
    targets = lax.dynamic_slice_in_dim(cell_points, offset, owned, 1)
    demag = source_field(targets, lax.all_gather(packed, "cell", axis=1, tiled=True))
    own_suscept = lax.dynamic_slice_in_dim(suscept, offset, owned, 0)
    updated = own_suscept[None, :] * (inducing[:, None] + demag)
    block_mag = lax.all_gather(updated, "stn", axis=1, tiled=True)
    moved = jnp.concatenate([cell_points, block_mag, size_h[None, :]], 0)
    field = source_field(stations, moved)
    predictions = lax.psum_scatter(
        jnp.sum(inducing[:, None] * field, axis=0), "cell", scatter_dimension=0, tiled=True
    )
    return (updated, predictions)


def solution(mesh):
    placed = (P(None, "cell"), P(None, "cell"), P("cell"), P("cell"), P(), P(None, "stn"))
    return jax.shard_map(
        shards,
        mesh=mesh,
        in_specs=placed,
        out_specs=(P(None, ("cell", "stn")), P(("stn", "cell"))),
        check_vma=False,
    )
```

profile of v0, /device:TPU:0, one launch (start us, length us, event | category | flops | bytes accessed | tf_op | source)
XLA Modules:
  0.0 82.9 jit_solution(14544340827631167878)
XLA Ops:
  0.6 0.7 constant_dynamic-slice_fusion.7
  1.3 0.7 multiply_multiply_fusion.3
  2.0 0.8 pad_maximum_fusion
  2.8 32.5 %all_gather.6 = f32[7,8192]{1,0:T(8,128)S(1)} all-gather(f32[7,1024]{1,0:T(8,128)S(1)} %pad_maximum_fusion), channel_id=1, replica_groups=mesh['cell'=8,'stn'=4] {'cell'}, dimensions={1}, use_global_device_ids=true | all-gather | bytes 258048 | tf_op jit(solution)/shard_map/all_gather | solution.py:62
  35.3 0.0 copy-start.3
  35.3 0.0 copy-start.2
  35.3 0.0 copy-start
  35.3 11.8 %while.3 = (s32[]{:T(128)}, f32[3,256]{1,0:T(4,128)S(1)}, f32[2,7,4096]{2,1,0:T(8,128)S(1)}, f32[3,256]{1,0:T(4,128)S(1)}, s32[]{:T(128)}, /*index=5*/s32[]{:T(128)}, s32[]{}, s32[]{}, s32[]{}, s32[]{}, /*index=10*/s32[]{}, s32[]{}) while((s32[]{:T(128)}, f32[3,256]{1,0:T(4,128)S(1)}, f32[2,7,4096]{2,1,0:T(8,128)S(1)}, ...), condition=%wide.region_4.5_spmd.clone, body=%wide.region_0.4_spmd.clone.sunk | while | flops 32524552 | bytes 431331 | solution.py:48
  35.3 0.1 constant_dynamic-slice_fusion.9
  35.5 5.7 %fusion.44 = (f32[256]{0:T(256)S(1)}, f32[256]{0:T(256)S(1)}, f32[256]{0:T(256)S(1)}) fusion(f32[4096]{0:T(1024)S(1)} %bitcast.60, f32[4096]{0:T(1024)S(1)} %bitcast.62, f32[256]{0:T(256)S(1)} %bitcast.69, f32[4096]{0:T(1024)S(1)} %get-tuple-element.134, f32[4096]{0:T(1024)S(1)} %bitcast.63, f32[4096]{0:T(1024)S(1)} %bitcast.61, f32[256]{0:T(256)S(1)} %bitcast.68, ...), kind=kLoop, calls=%fused_computation.19.clone.1 | loop fusion | flops 32505088 | bytes 137216 | tf_op jit(solution)/shard_map/while/body/eval_jaxpr/reduce_sum | solution.py:34
  41.2 0.1 constant_dynamic-slice_fusion.9
  41.4 5.7 %fusion.44 = (f32[256]{0:T(256)S(1)}, f32[256]{0:T(256)S(1)}, f32[256]{0:T(256)S(1)}) fusion(f32[4096]{0:T(1024)S(1)} %bitcast.60, f32[4096]{0:T(1024)S(1)} %bitcast.62, f32[256]{0:T(256)S(1)} %bitcast.69, f32[4096]{0:T(1024)S(1)} %get-tuple-element.134, f32[4096]{0:T(1024)S(1)} %bitcast.63, f32[4096]{0:T(1024)S(1)} %bitcast.61, f32[256]{0:T(256)S(1)} %bitcast.68, ...), kind=kLoop, calls=%fused_computation.19.clone.1 | loop fusion | flops 32505088 | bytes 137216 | tf_op jit(solution)/shard_map/while/body/eval_jaxpr/reduce_sum | solution.py:34
  47.2 0.8 dynamic_slice.13
  47.9 0.0 copy-done.3
  47.9 0.1 add_multiply_fusion
  48.0 0.0 copy-start.1
  48.0 5.2 %all_gather.7 = f32[3,1024]{1,0:T(4,128)S(1)} all-gather(f32[3,256]{1,0:T(4,128)S(1)} %add_multiply_fusion), channel_id=1, replica_groups=mesh['cell'=8,'stn'=4] {'stn'}, dimensions={1}, use_global_device_ids=true | all-gather | bytes 15360 | tf_op jit(solution)/shard_map/all_gather | solution.py:65
  53.2 0.0 copy-done.2
  53.2 0.0 copy-done
  53.2 0.0 copy-start.4
  53.3 6.2 %fusion.27 = (f32[1024]{0:T(1024)S(1)}, f32[1024]{0:T(1024)S(1)}, f32[1024]{0:T(1024)S(1)}) fusion(f32[1024]{0:T(1024)S(1)} %bitcast.73, f32[1024]{0:T(1024)S(1)} %bitcast.78, f32[1024]{0:T(1024)S(1)} %bitcast.75, f32[1024]{0:T(1024)S(1)} %get-tuple-element.88, f32[1024]{0:T(1024)S(1)} %bitcast.72, f32[1024]{0:T(1024)S(1)} %bitcast.79, ...), kind=kLoop, calls=%fused_computation.55 | loop fusion | flops 32502784 | bytes 57344 | tf_op jit(solution)/shard_map/while/body/eval_jaxpr/reduce_sum | solution.py:34
  59.5 0.0 copy-done.1
  59.5 0.1 fusion.34
  59.6 21.4 %all-reduce = f32[1024]{0:T(1024)S(1)} all-reduce(f32[1024]{0:T(1024)S(1)} %fusion.34), channel_id=2, replica_groups=mesh['cell'=8,'stn'=4] {'cell'}, use_global_device_ids=true, to_apply=%region_9.10.clone | all-reduce | flops 1024 | bytes 8192
  81.0 0.0 copy-done.4
  81.0 0.6 dynamic-slice.1
  82.3 0.6 dynamic-slice.2
  (10 shorter events, 0.1 us)
Async XLA Ops:
  35.3 12.6 %copy-start.3 = (f32[3]{0:T(128)S(1)}, f32[3]{0:T(128)}, u32[]{:S(2)}) copy-start(f32[3]{0:T(128)} %param.12) | copy-start | bytes 40
  35.3 17.9 %copy-start.2 = (f32[3,1024]{1,0:T(4,128)S(1)}, f32[3,1024]{1,0:T(4,128)}, u32[]{:S(2)}) copy-start(f32[3,1024]{1,0:T(4,128)} %param.13) | copy-start | bytes 36868
  35.3 17.9 %copy-start = (f32[3,1024]{1,0:T(4,128)S(1)}, f32[3,1024]{1,0:T(4,128)}, u32[]{:S(2)}) copy-start(f32[3,1024]{1,0:T(4,128)} %param.8) | copy-start | bytes 36868
  48.0 11.5 %copy-start.1 = (f32[3,256]{1,0:T(4,128)}, f32[3,256]{1,0:T(4,128)S(1)}, u32[]{:S(2)}) copy-start(f32[3,256]{1,0:T(4,128)S(1)} %add_multiply_fusion) | copy-start | bytes 9220
  53.2 27.8 %copy-start.4 = (u32[32]{0:T(128)S(1)}, u32[32]{0:T(128)}, u32[]{:S(2)}) copy-start(u32[32]{0:T(128)} %constant.48) | copy-start | bytes 388
where the time goes:
time: 83.3 us; the launch traced here: 82.9 us
  blocking collectives  59.1 us (71%)
  other arithmetic  19.4 us (23%)
  local copies, waits for them, and re-layouts  2.93 us (4%)
  between operations  1.37 us (2%)
    all_gather x1, blocking collectives, shards(): lax.all_gather(packed, 'cell', axis=1, tiled=True)  32.5 us
    unnamed x1, blocking collectives  21.4 us
    reduce_sum x3, other arithmetic, pair_field(): jnp.sum(weight * (projection * delta_x - source_piece[3][None, :]), axis=1)  17.7 us
    all_gather x1, blocking collectives, shards(): block_mag = lax.all_gather(updated, 'stn', axis=1, tiled=True)  5.17 us

commit v1 on v0

--- a/solution.py
+++ b/solution.py
@@ -5,6 +5,16 @@
 from jax.sharding import PartitionSpec as P
 
 INV_FOUR_PI = 0.25 / math.pi
+
+
+def around_the_ring(x, name, dim):
+    n_dev = lax.axis_size(name)
+    held, blocks = (x, [x])
+    for _ in range(n_dev - 1):
+        held = lax.ppermute(held, name, [(i, (i + 1) % n_dev) for i in range(n_dev)])
+        blocks.insert(0, held)
+    flat = jnp.concatenate(blocks, axis=dim)
+    return jnp.roll(flat, (lax.axis_index(name) + 1) * x.shape[dim], axis=dim)
 
 
 def block_width(targets, sources):
@@ -62,7 +72,7 @@
     demag = source_field(targets, lax.all_gather(packed, "cell", axis=1, tiled=True))
     own_suscept = lax.dynamic_slice_in_dim(suscept, offset, owned, 0)
     updated = own_suscept[None, :] * (inducing[:, None] + demag)
-    block_mag = lax.all_gather(updated, "stn", axis=1, tiled=True)
+    block_mag = around_the_ring(updated, "stn", 1)
     moved = jnp.concatenate([cell_points, block_mag, size_h[None, :]], 0)
     field = source_field(stations, moved)
     predictions = lax.psum_scatter(

time: 83.3 us -> 86.2 us (1.035)
  waiting for transfers between devices: 0 us -> 7.79 us
  blocking collectives: 59.1 us -> 54 us
    ppermute x0 -> x3, waiting for transfers between devices: none -> 7.79 us  [around_the_ring(): lax.ppermute(held, name, [(i, (i + 1) % n_dev) for i in range(n_dev)])]
    all_gather x1 -> x0, blocking collectives: 5.17 us -> none  [shards(): block_mag = lax.all_gather(updated, 'stn', axis=1, tiled=True)]
  transfers between devices with their start and end apart: 0 -> 3, of which waited for: 0 -> 3; matrix products, arithmetic and copies ran while one was open for 0% -> 1% of each run, Pallas kernels for 0% -> 0%
where the time goes in v1:
time: 86.2 us; the launch traced here: 85.7 us
  blocking collectives  54 us (63%)
  other arithmetic  19.5 us (23%)
  waiting for transfers between devices  7.79 us (9%)
  local copies, waits for them, and re-layouts  3.04 us (4%)
  between operations  1.38 us (2%)
    all_gather x1, blocking collectives, shards(): lax.all_gather(packed, 'cell', axis=1, tiled=True)  32.5 us
    unnamed x1, blocking collectives  21.4 us
    reduce_sum x3, other arithmetic, pair_field(): jnp.sum(weight * (projection * delta_x - source_piece[3][None, :]), axis=1)  17.7 us
    ppermute x3, waiting for transfers between devices, around_the_ring(): lax.ppermute(held, name, [(i, (i + 1) % n_dev) for i in range(n_dev)])  7.79 us
  transfers between devices with their start and end apart: 3, of which 3 were waited for; matrix products, arithmetic and copies ran while one was open for 1% of the time, Pallas kernels for 0%

profile of v1, /device:TPU:0, one launch (start us, length us, event | category | flops | bytes accessed | tf_op | source)
XLA Modules:
  0.0 85.7 jit_solution(4546358705420506428)
XLA Ops:
  0.6 0.7 multiply_multiply_fusion.3
  1.3 0.7 constant_dynamic-slice_fusion.8
  2.0 0.8 pad_maximum_fusion
  2.8 32.5 %all_gather.3 = f32[7,8192]{1,0:T(8,128)S(1)} all-gather(f32[7,1024]{1,0:T(8,128)S(1)} %pad_maximum_fusion), channel_id=1, replica_groups=mesh['cell'=8,'stn'=4] {'cell'}, dimensions={1}, use_global_device_ids=true | all-gather | bytes 258048 | tf_op jit(solution)/shard_map/all_gather | solution.py:72
  35.3 0.0 copy-start.2
  35.3 0.0 copy-start
  35.3 0.0 copy-start.1
  35.3 0.0 copy-start.4
  35.3 11.8 %while.3 = (s32[]{:T(128)}, f32[3,256]{1,0:T(4,128)S(1)}, f32[2,7,4096]{2,1,0:T(8,128)S(1)}, f32[3,256]{1,0:T(4,128)S(1)}, s32[]{:T(128)}, /*index=5*/s32[]{:T(128)}, s32[]{}, s32[]{}, s32[]{}, s32[]{}, /*index=10*/s32[]{}, s32[]{}) while((s32[]{:T(128)}, f32[3,256]{1,0:T(4,128)S(1)}, f32[2,7,4096]{2,1,0:T(8,128)S(1)}, ...), condition=%wide.region_4.5_spmd.clone, body=%wide.region_0.4_spmd.clone.sunk | while | flops 32524552 | bytes 431331 | solution.py:58
  35.3 0.1 constant_dynamic-slice_fusion.10
  35.5 5.7 %fusion.44 = (f32[256]{0:T(256)S(1)}, f32[256]{0:T(256)S(1)}, f32[256]{0:T(256)S(1)}) fusion(f32[4096]{0:T(1024)S(1)} %bitcast.60, f32[4096]{0:T(1024)S(1)} %bitcast.62, f32[256]{0:T(256)S(1)} %bitcast.69, f32[4096]{0:T(1024)S(1)} %get-tuple-element.134, f32[4096]{0:T(1024)S(1)} %bitcast.63, f32[4096]{0:T(1024)S(1)} %bitcast.61, f32[256]{0:T(256)S(1)} %bitcast.68, ...), kind=kLoop, calls=%fused_computation.19.clone.1 | loop fusion | flops 32505088 | bytes 137216 | tf_op jit(solution)/shard_map/while/body/eval_jaxpr/reduce_sum | solution.py:44
  41.3 0.1 constant_dynamic-slice_fusion.10
  41.4 5.7 %fusion.44 = (f32[256]{0:T(256)S(1)}, f32[256]{0:T(256)S(1)}, f32[256]{0:T(256)S(1)}) fusion(f32[4096]{0:T(1024)S(1)} %bitcast.60, f32[4096]{0:T(1024)S(1)} %bitcast.62, f32[256]{0:T(256)S(1)} %bitcast.69, f32[4096]{0:T(1024)S(1)} %get-tuple-element.134, f32[4096]{0:T(1024)S(1)} %bitcast.63, f32[4096]{0:T(1024)S(1)} %bitcast.61, f32[256]{0:T(256)S(1)} %bitcast.68, ...), kind=kLoop, calls=%fused_computation.19.clone.1 | loop fusion | flops 32505088 | bytes 137216 | tf_op jit(solution)/shard_map/while/body/eval_jaxpr/reduce_sum | solution.py:44
  47.2 0.8 dynamic_slice.17
  47.9 0.0 copy-done.2
  47.9 0.1 add_multiply_fusion
  48.0 0.0 copy-start.3
  48.0 0.0 collective-permute-start
  48.0 3.0 %collective-permute-done = f32[3,256]{1,0:T(4,128)S(1)} collective-permute-done((f32[3,256]{1,0:T(4,128)S(1)}, f32[3,256]{1,0:T(4,128)S(1)}, u32[]{:S(2)}, u32[]{:S(2)}) %collective-permute-start) | collective-permute-done | bytes 3104 | tf_op jit(solution)/shard_map/ppermute | solution.py:14
  51.1 0.0 collective-permute-start.1
  51.1 0.0 copy-done
  51.1 3.0 %collective-permute-done.1 = f32[3,256]{1,0:T(4,128)S(1)} collective-permute-done((f32[3,256]{1,0:T(4,128)S(1)}, f32[3,256]{1,0:T(4,128)S(1)}, u32[]{:S(2)}, u32[]{:S(2)}) %collective-permute-start.1) | collective-permute-done | bytes 3104 | tf_op jit(solution)/shard_map/ppermute | solution.py:14
  54.1 0.0 collective-permute-start.2
  54.1 0.0 copy-done.1
  54.1 0.0 copy-done.4
  54.1 0.6 dynamic-slice.1
  55.4 1.7 %collective-permute-done.2 = f32[3,256]{1,0:T(4,128)S(1)} collective-permute-done((f32[3,256]{1,0:T(4,128)S(1)}, f32[3,256]{1,0:T(4,128)S(1)}, u32[]{:S(2)}, u32[]{:S(2)}) %collective-permute-start.2) | collective-permute-done | bytes 3104 | tf_op jit(solution)/shard_map/ppermute | solution.py:14
  57.1 0.1 constant_dynamic-update-slice_fusion.4
  57.2 0.1 constant_dynamic-update-slice_fusion
  57.3 0.1 fusion.38
  57.4 6.2 %fusion.27 = (f32[1024]{0:T(1024)S(1)}, f32[1024]{0:T(1024)S(1)}, f32[1024]{0:T(1024)S(1)}) fusion(f32[1024]{0:T(1024)S(1)} %bitcast.72, f32[1024]{0:T(1024)S(1)} %bitcast.75, f32[1024]{0:T(1024)S(1)} %bitcast.78, f32[1024]{0:T(1024)S(1)} %get-tuple-element.88, f32[1024]{0:T(1024)S(1)} %bitcast.73, f32[1024]{0:T(1024)S(1)} %bitcast.76, ...), kind=kLoop, calls=%fused_computation.55 | loop fusion | flops 32502784 | bytes 57344 | tf_op jit(solution)/shard_map/while/body/eval_jaxpr/reduce_sum | solution.py:44
  63.6 0.0 copy-done.3
  63.6 0.1 fusion.34
  63.7 21.4 %all-reduce = f32[1024]{0:T(1024)S(1)} all-reduce(f32[1024]{0:T(1024)S(1)} %fusion.34), channel_id=2, replica_groups=mesh['cell'=8,'stn'=4] {'cell'}, use_global_device_ids=true, to_apply=%region_9.10.clone | all-reduce | flops 1024 | bytes 8192
  85.1 0.6 dynamic-slice.2
  (15 shorter events, 0.1 us)
Async XLA Ops:
  35.3 12.6 %copy-start.2 = (f32[3]{0:T(128)S(1)}, f32[3]{0:T(128)}, u32[]{:S(2)}) copy-start(f32[3]{0:T(128)} %param.12) | copy-start | bytes 40
  35.3 15.7 %copy-start = (f32[3,1024]{1,0:T(4,128)S(1)}, f32[3,1024]{1,0:T(4,128)}, u32[]{:S(2)}) copy-start(f32[3,1024]{1,0:T(4,128)} %param.8) | copy-start | bytes 36868
  35.3 18.8 %copy-start.1 = (f32[3,1024]{1,0:T(4,128)S(1)}, f32[3,1024]{1,0:T(4,128)}, u32[]{:S(2)}) copy-start(f32[3,1024]{1,0:T(4,128)} %param.13) | copy-start | bytes 36868
  35.3 18.8 %copy-start.4 = (u32[32]{0:T(128)S(1)}, u32[32]{0:T(128)}, u32[]{:S(2)}) copy-start(u32[32]{0:T(128)} %constant.70) | copy-start | bytes 388
  48.0 15.6 %copy-start.3 = (f32[3,256]{1,0:T(4,128)}, f32[3,256]{1,0:T(4,128)S(1)}, u32[]{:S(2)}) copy-start(f32[3,256]{1,0:T(4,128)S(1)} %add_multiply_fusion) | copy-start | bytes 9220
  48.0 3.0 %collective-permute-start = (f32[3,256]{1,0:T(4,128)S(1)}, f32[3,256]{1,0:T(4,128)S(1)}, u32[]{:S(2)}, u32[]{:S(2)}) collective-permute-start(f32[3,256]{1,0:T(4,128)S(1)} %add_multiply_fusion), channel_id=1, source_target_pairs={{0,1},{1,2},{2,3},{3,0},{4,5},{5,6},{6,7},{7,4},{8,9},{9,10},{10,1... | collective-permute-start | bytes 9224 | tf_op jit(solution)/shard_map/ppermute | solution.py:14
  51.1 3.0 %collective-permute-start.1 = (f32[3,256]{1,0:T(4,128)S(1)}, f32[3,256]{1,0:T(4,128)S(1)}, u32[]{:S(2)}, u32[]{:S(2)}) collective-permute-start(f32[3,256]{1,0:T(4,128)S(1)} %collective-permute-done), channel_id=1, source_target_pairs={{0,1},{1,2},{2,3},{3,0},{4,5},{5,6},{6,7},{7,4},{8,9},{9,10},{10,1... | collective-permute-start | bytes 9224 | tf_op jit(solution)/shard_map/ppermute | solution.py:14
  54.1 3.0 %collective-permute-start.2 = (f32[3,256]{1,0:T(4,128)S(1)}, f32[3,256]{1,0:T(4,128)S(1)}, u32[]{:S(2)}, u32[]{:S(2)}) collective-permute-start(f32[3,256]{1,0:T(4,128)S(1)} %collective-permute-done.1), channel_id=1, source_target_pairs={{0,1},{1,2},{2,3},{3,0},{4,5},{5,6},{6,7},{7,4},{8,9},{9,10},{10,1... | collective-permute-start | bytes 9224 | tf_op jit(solution)/shard_map/ppermute | solution.py:14
